TPU v7x, 512 devices: a whole 4x8x8 slice. The times are simulated.
512 devices in a mesh: feat: 64 (over y_lo, z, core), grp: 8 (over x, y_hi).
Axes of the slice: x: 4, y: 8 (y_hi: 2, y_lo: 4; y = y_hi * 4 + y_lo), z: 8, core: 2. Of those that a mesh axis runs over, the one named last changes fastest.
Arguments:
- gradients: bfloat16 [8, 16777216], P('grp', 'feat'), may hold values from -6 to 6
- sign_bits: int32 [16777216], P('feat'), may hold values 0 or 1
- kept_rows: int32 [16384], replicated, may hold values from 0 to 16777215
- queries: bfloat16 [512, 16384], P('grp', 'feat'), may hold values from -0.046875 to 0.046875
Outputs:
- projections: bfloat16 [8, 16384], P('grp', 'feat')
- scores: float32 [8, 512], P('grp', 'feat')
All inputs are finite; a program needn't handle non-finite values. No bound on the sum of `sign_bits` on one device may be relied on, other than what follows from the above.
Results may differ from a plain program's by a relative error of at most 0.0057.
Values may be sent and summed in bfloat16 or wider, within the bound.
A program may use at most 64 MiB of HBM per device.

v0:
```python
import math

import jax
import jax.numpy as jnp
from jax import lax
from jax.sharding import PartitionSpec as P


def from_behind(array, axis, by):
    length = lax.axis_size(axis)
    return lax.ppermute(array, axis, [(i, (i + by) % length) for i in range(length)])


def parity_sign(first_index, second_index, bit_count):
    common = jnp.bitwise_and(first_index, second_index)
    oddity = jnp.zeros_like(common)
    for bit_pos in range(bit_count):
        oddity = jnp.bitwise_xor(oddity, jnp.bitwise_and(jnp.right_shift(common, bit_pos), 1))
    return (1 - 2 * oddity).astype(jnp.float32)


def hadamard_table(length):
    counter = jnp.arange(length, dtype=jnp.int32)
    return parity_sign(counter[:, None], counter[None, :], max(length.bit_length() - 1, 1))


def on_device(gradients, sign_bits, kept_rows, queries):
    devices = lax.axis_size("feat")
    position = lax.axis_index("feat")
    examples, local_len = gradients.shape
    total_bits = local_len.bit_length() - 1
    inner_len = 1 << total_bits // 2
    outer_len = local_len // inner_len
    per_device = kept_rows.shape[0] // devices
    table_inner = hadamard_table(inner_len).astype(jnp.bfloat16)
    table_outer = hadamard_table(outer_len).astype(jnp.bfloat16)
    table_device = hadamard_table(devices).astype(jnp.bfloat16)
    flipped = jnp.where(sign_bits == 1, -gradients, gradients).reshape(
        examples, outer_len, inner_len
    )
    section_one = (
        jnp.einsum("eab,cb->eac", flipped, table_inner, preferred_element_type=jnp.float32)
        / math.sqrt(inner_len)
    ).astype(jnp.bfloat16)
    section_two = (
        jnp.einsum("eab,ca->ecb", section_one, table_outer, preferred_element_type=jnp.float32)
        / math.sqrt(outer_len)
    ).astype(jnp.bfloat16)
    mixed_local = section_two.reshape(examples, local_len)
    own_rows = (
        lax.dynamic_slice_in_dim(kept_rows, position * per_device, per_device)
        - position * local_len
    )
    summed = jnp.einsum(
        "edm,jd->ejm",
        lax.all_to_all(
            mixed_local.reshape(examples, devices, local_len // devices),
            "feat",
            split_axis=1,
            concat_axis=1,
            tiled=True,
        ),
        table_device,
        preferred_element_type=jnp.float32,
    ) / math.sqrt(devices)
    rounded = summed.astype(jnp.bfloat16)
    returned = lax.all_to_all(rounded, "feat", split_axis=1, concat_axis=1, tiled=True)
    projections = returned.reshape(returned.shape[0], local_len)[:, own_rows]
    groups = lax.axis_size("grp")
    block_rows = queries.shape[0]
    group_pos = lax.axis_index("grp")
    collected = jnp.zeros((examples, block_rows * groups), jnp.float32)
    travelling = queries
    for stop_index in range(groups):
        source = (group_pos - stop_index) % groups * block_rows
        collected = lax.dynamic_update_slice(
            collected,
            lax.dot_general(
                projections,
                travelling,
                (((1,), (1,)), ((), ())),
                preferred_element_type=jnp.float32,
            ),
            (jnp.int32(0), source),
        )
        if stop_index + 1 < groups:
            travelling = from_behind(travelling, "grp", 1)
    scores = lax.psum_scatter(collected, "feat", scatter_dimension=1, tiled=True)
    return (projections, scores)


def solution(mesh):
    in_specs = (P("grp", "feat"), P("feat"), P(), P("grp", "feat"))
    out_specs = (P("grp", "feat"), P("grp", "feat"))
    return jax.shard_map(
        on_device, mesh=mesh, in_specs=in_specs, out_specs=out_specs, check_vma=False
    )
```

profile of v0, /device:TPU:1, one launch (start us, length us, event | category | flops | bytes accessed | tf_op | source)
XLA Modules:
  0.0 285.8 jit_solution(17988946352981790317)
XLA Ops:
  0.6 0.0 copy-start
  0.6 1.5 broadcast_compare_fusion
  2.1 0.1 copy-done
  2.2 9.3 %fusion.4 = bf16[262144]{0:T(1024)(128)(2,1)S(1)} fusion(bf16[1,262144]{1,0:T(2,128)(2,1)S(1)} %copy-done, pred[262144]{0:T(1024)(128)(4,1)S(1)} %broadcast_compare_fusion), kind=kLoop, calls=%fused_computation.10 | loop fusion | flops 1048576 | bytes 1310720 | tf_op jit(solution)/shard_map/jit(_where)/select_n | solution.py:38
  11.5 0.3 reshape.47
  11.8 1.7 fusion.3
  13.5 0.3 reshape_reshape.4
  13.8 0.5 broadcast.143
  14.4 3.8 %reduce.4 = bf16[64,4096]{1,0:T(8,128)(2,1)S(1)} reduce(bf16[64,1,4096]{2,1,0:T(2,128)(2,1)S(1)} %bitcast.42, bf16[]{:T(256)} %broadcast.143), dimensions={1}, to_apply=%bitcast.18.reduce_sub_computation | reduce | bytes 1048578
  18.2 0.4 reshape.85
  18.5 32.4 %all_to_all.10 = bf16[64,2,2048]{2,1,0:T(2,128)(2,1)S(1)} all-to-all(bf16[64,2,2048]{2,1,0:T(2,128)(2,1)S(1)} %reshape.85), channel_id=1, replica_groups=mesh['feat'=64,'grp'=8] {'feat'}, dimensions={0} | all-to-all | bytes 1048576 | tf_op jit(solution)/shard_map/all_to_all | solution.py:56
  50.9 0.5 reshape.86
  51.4 0.8 fusion.1
  52.2 1.2 copy.19
  53.4 3.8 %reduce.5 = bf16[64,4096]{1,0:T(8,128)(2,1)S(1)} reduce(bf16[64,1,4096]{2,1,0:T(2,128)(2,1)S(1)} %bitcast.43, bf16[]{:T(256)} %broadcast.143), dimensions={1}, to_apply=%bitcast.41.reduce_sub_computation | reduce | bytes 1048578
  57.2 1.2 reshape.87
  58.3 0.0 copy-start.1
  58.3 6.2 %all-to-all-start.1 = ((bf16[64,2,2048]{2,1,0:T(2,128)(2,1)}), bf16[64,2,2048]{2,1,0:T(2,128)(2,1)S(1)}, u32[]{:S(2)}, u32[]{:S(2)}) async-start(bf16[64,2,2048]{2,1,0:T(2,128)(2,1)} %reshape.87), calls=%async_computation.1 | async-start | bytes 1048576 | tf_op jit(solution)/shard_map/all_to_all | solution.py:67
  64.6 0.0 copy-done.1
  64.6 4.8 %collective-permute-start = (bf16[64,256]{1,0:T(8,128)(2,1)S(1)}, bf16[64,256]{1,0:T(8,128)(2,1)S(1)}, u32[]{:S(2)}, u32[]{:S(2)}) collective-permute-start(bf16[64,256]{1,0:T(8,128)(2,1)S(1)} %copy-done.1), channel_id=1, source_target_pairs={{0,1},{1,2},{2,3},{3,4},{4,5},{5,6},{6,7},{7,0},{8,9},{9,10},{10,1... | collective-permute-start | bytes 98312 | tf_op jit(solution)/shard_map/ppermute | solution.py:11
  69.3 9.9 %collective-permute-done = bf16[64,256]{1,0:T(8,128)(2,1)S(1)} collective-permute-done((bf16[64,256]{1,0:T(8,128)(2,1)S(1)}, bf16[64,256]{1,0:T(8,128)(2,1)S(1)}, u32[]{:S(2)}, u32[]{:S(2)}) %collective-permute-start) | collective-permute-done | bytes 32800 | tf_op jit(solution)/shard_map/ppermute | solution.py:11
  79.3 2.5 collective-permute-start.1
  81.7 8.5 %collective-permute-done.1 = bf16[64,256]{1,0:T(8,128)(2,1)S(1)} collective-permute-done((bf16[64,256]{1,0:T(8,128)(2,1)S(1)}, bf16[64,256]{1,0:T(8,128)(2,1)S(1)}, u32[]{:S(2)}, u32[]{:S(2)}) %collective-permute-start.1) | collective-permute-done | bytes 32800 | tf_op jit(solution)/shard_map/ppermute | solution.py:11
  90.3 1.9 collective-permute-start.2
  92.2 8.7 %collective-permute-done.2 = bf16[64,256]{1,0:T(8,128)(2,1)S(1)} collective-permute-done((bf16[64,256]{1,0:T(8,128)(2,1)S(1)}, bf16[64,256]{1,0:T(8,128)(2,1)S(1)}, u32[]{:S(2)}, u32[]{:S(2)}) %collective-permute-start.2) | collective-permute-done | bytes 32800 | tf_op jit(solution)/shard_map/ppermute | solution.py:11
  100.9 1.9 collective-permute-start.3
  102.9 8.7 %collective-permute-done.3 = bf16[64,256]{1,0:T(8,128)(2,1)S(1)} collective-permute-done((bf16[64,256]{1,0:T(8,128)(2,1)S(1)}, bf16[64,256]{1,0:T(8,128)(2,1)S(1)}, u32[]{:S(2)}, u32[]{:S(2)}) %collective-permute-start.3) | collective-permute-done | bytes 32800 | tf_op jit(solution)/shard_map/ppermute | solution.py:11
  111.6 1.9 collective-permute-start.4
  113.5 0.8 compare_select_fusion
  114.3 8.0 %collective-permute-done.4 = bf16[64,256]{1,0:T(8,128)(2,1)S(1)} collective-permute-done((bf16[64,256]{1,0:T(8,128)(2,1)S(1)}, bf16[64,256]{1,0:T(8,128)(2,1)S(1)}, u32[]{:S(2)}, u32[]{:S(2)}) %collective-permute-start.4) | collective-permute-done | bytes 32800 | tf_op jit(solution)/shard_map/ppermute | solution.py:11
  122.3 1.9 collective-permute-start.5
  124.4 1.3 dynamic-slice
  126.3 6.7 %collective-permute-done.5 = bf16[64,256]{1,0:T(8,128)(2,1)S(1)} collective-permute-done((bf16[64,256]{1,0:T(8,128)(2,1)S(1)}, bf16[64,256]{1,0:T(8,128)(2,1)S(1)}, u32[]{:S(2)}, u32[]{:S(2)}) %collective-permute-start.5) | collective-permute-done | bytes 32800 | tf_op jit(solution)/shard_map/ppermute | solution.py:11
  132.9 2.1 collective-permute-start.6
  135.1 0.0 all-to-all-done.1
  135.1 0.5 reshape.88
  135.6 3.1 %bitcast_reduce_fusion = bf16[64,4096]{1,0:T(8,128)(2,1)S(1)} fusion(bf16[64,1,4096]{2,1,0:T(2,128)(2,1)S(1)} %reshape.88), kind=kLoop, calls=%fused_computation.50 | loop fusion | bytes 1048576 | tf_op jit(solution)/shard_map/all_to_all | solution.py:67
  138.7 0.1 copy.13
  138.8 1.9 gather_fusion
  140.8 0.1 fusion.57
  140.9 0.1 fusion.58
  141.0 0.1 fusion.59
  141.1 0.1 fusion.60
  141.2 0.1 fusion.61
  141.4 0.1 fusion.62
  141.5 0.1 fusion.63
  141.6 0.6 reshape.52
  142.3 0.1 dynamic_update_slice.24
  142.3 0.3 dynamic_update_slice.25
  142.6 0.1 dynamic_update_slice.26
  142.7 0.3 dynamic_update_slice.27
  143.0 0.1 dynamic_update_slice.28
  143.1 0.3 dynamic_update_slice.29
  143.4 0.1 dynamic_update_slice.30
  143.6 0.0 collective-permute-done.6
  143.6 0.1 fusion.64
  143.7 0.2 dynamic_update_slice.31
  143.9 141.4 %all-reduce = f32[1,512]{1,0:T(1,128)S(1)} all-reduce(f32[1,512]{1,0:T(1,128)S(1)} %dynamic_update_slice.31), channel_id=2, replica_groups=mesh['feat'=64,'grp'=8] {'feat'}, use_global_device_ids=true, to_apply=%region_0.1.clone | all-reduce | flops 512 | bytes 4096
  285.3 0.6 constant_dynamic-slice_fusion
  (3 shorter events, 0.0 us)
Async XLA Ops:
  0.6 1.5 copy-start
  58.3 6.2 %copy-start.1 = (bf16[64,256]{1,0:T(8,128)(2,1)S(1)}, bf16[64,256]{1,0:T(8,128)(2,1)}, u32[]{:S(2)}) copy-start(bf16[64,256]{1,0:T(8,128)(2,1)} %param.7) | copy-start | bytes 98308
  58.3 76.7 %all-to-all-start.1 = ((bf16[64,2,2048]{2,1,0:T(2,128)(2,1)}), bf16[64,2,2048]{2,1,0:T(2,128)(2,1)S(1)}, u32[]{:S(2)}, u32[]{:S(2)}) async-start(bf16[64,2,2048]{2,1,0:T(2,128)(2,1)} %reshape.87), calls=%async_computation.1 | async-start | bytes 1048576 | tf_op jit(solution)/shard_map/all_to_all | solution.py:67
  64.6 14.7 %collective-permute-start = (bf16[64,256]{1,0:T(8,128)(2,1)S(1)}, bf16[64,256]{1,0:T(8,128)(2,1)S(1)}, u32[]{:S(2)}, u32[]{:S(2)}) collective-permute-start(bf16[64,256]{1,0:T(8,128)(2,1)S(1)} %copy-done.1), channel_id=1, source_target_pairs={{0,1},{1,2},{2,3},{3,4},{4,5},{5,6},{6,7},{7,0},{8,9},{9,10},{10,1... | collective-permute-start | bytes 98312 | tf_op jit(solution)/shard_map/ppermute | solution.py:11
  79.3 11.0 %collective-permute-start.1 = (bf16[64,256]{1,0:T(8,128)(2,1)S(1)}, bf16[64,256]{1,0:T(8,128)(2,1)S(1)}, u32[]{:S(2)}, u32[]{:S(2)}) collective-permute-start(bf16[64,256]{1,0:T(8,128)(2,1)S(1)} %collective-permute-done), channel_id=1, source_target_pairs={{0,1},{1,2},{2,3},{3,4},{4,5},{5,6},{6,7},{7,0},{8,9},{9,10},{10,1... | collective-permute-start | bytes 98312 | tf_op jit(solution)/shard_map/ppermute | solution.py:11
  90.3 10.7 %collective-permute-start.2 = (bf16[64,256]{1,0:T(8,128)(2,1)S(1)}, bf16[64,256]{1,0:T(8,128)(2,1)S(1)}, u32[]{:S(2)}, u32[]{:S(2)}) collective-permute-start(bf16[64,256]{1,0:T(8,128)(2,1)S(1)} %collective-permute-done.1), channel_id=1, source_target_pairs={{0,1},{1,2},{2,3},{3,4},{4,5},{5,6},{6,7},{7,0},{8,9},{9,10},{10,1... | collective-permute-start | bytes 98312 | tf_op jit(solution)/shard_map/ppermute | solution.py:11
  100.9 10.7 %collective-permute-start.3 = (bf16[64,256]{1,0:T(8,128)(2,1)S(1)}, bf16[64,256]{1,0:T(8,128)(2,1)S(1)}, u32[]{:S(2)}, u32[]{:S(2)}) collective-permute-start(bf16[64,256]{1,0:T(8,128)(2,1)S(1)} %collective-permute-done.2), channel_id=1, source_target_pairs={{0,1},{1,2},{2,3},{3,4},{4,5},{5,6},{6,7},{7,0},{8,9},{9,10},{10,1... | collective-permute-start | bytes 98312 | tf_op jit(solution)/shard_map/ppermute | solution.py:11
  111.6 10.7 %collective-permute-start.4 = (bf16[64,256]{1,0:T(8,128)(2,1)S(1)}, bf16[64,256]{1,0:T(8,128)(2,1)S(1)}, u32[]{:S(2)}, u32[]{:S(2)}) collective-permute-start(bf16[64,256]{1,0:T(8,128)(2,1)S(1)} %collective-permute-done.3), channel_id=1, source_target_pairs={{0,1},{1,2},{2,3},{3,4},{4,5},{5,6},{6,7},{7,0},{8,9},{9,10},{10,1... | collective-permute-start | bytes 98312 | tf_op jit(solution)/shard_map/ppermute | solution.py:11
  122.3 10.7 %collective-permute-start.5 = (bf16[64,256]{1,0:T(8,128)(2,1)S(1)}, bf16[64,256]{1,0:T(8,128)(2,1)S(1)}, u32[]{:S(2)}, u32[]{:S(2)}) collective-permute-start(bf16[64,256]{1,0:T(8,128)(2,1)S(1)} %collective-permute-done.4), channel_id=1, source_target_pairs={{0,1},{1,2},{2,3},{3,4},{4,5},{5,6},{6,7},{7,0},{8,9},{9,10},{10,1... | collective-permute-start | bytes 98312 | tf_op jit(solution)/shard_map/ppermute | solution.py:11
  132.9 10.7 %collective-permute-start.6 = (bf16[64,256]{1,0:T(8,128)(2,1)S(1)}, bf16[64,256]{1,0:T(8,128)(2,1)S(1)}, u32[]{:S(2)}, u32[]{:S(2)}) collective-permute-start(bf16[64,256]{1,0:T(8,128)(2,1)S(1)} %collective-permute-done.5), channel_id=1, source_target_pairs={{0,1},{1,2},{2,3},{3,4},{4,5},{5,6},{6,7},{7,0},{8,9},{9,10},{10,1... | collective-permute-start | bytes 98312 | tf_op jit(solution)/shard_map/ppermute | solution.py:11
where the time goes:
time: 286 us
  blocking collectives  174 us (61%)
  waiting for transfers between devices  50.6 us (18%)
  starting transfers between devices  23.2 us (8%)
  other arithmetic  19.1 us (7%)
  local copies, waits for them, and re-layouts  14.1 us (5%)
  matrix products  3.43 us (1%)
    unnamed x1, blocking collectives  141 us
    ppermute x7, waiting for transfers between devices, from_behind(): lax.ppermute(array, axis, [(i, (i + by) % length) for i in range(length)])  50.6 us
    all_to_all x1, blocking collectives, on_device(): lax.all_to_all(mixed_local.reshape(examples, devices, local_len // device...  32.4 us
    ppermute x7, starting transfers between devices, from_behind(): lax.ppermute(array, axis, [(i, (i + by) % length) for i in range(length)])  17 us
    select_n x1, other arithmetic, on_device(): jnp.where(sign_bits == 1, -gradients, gradients)  9.29 us
    unnamed x2, other arithmetic  7.59 us
    all_to_all x1, starting transfers between devices, on_device(): lax.all_to_all(rounded, 'feat', split_axis=1, concat_axis=1, tiled=True)  6.2 us
  transfers between devices with their start and end apart: 8, of which 6 were waited for; matrix products, arithmetic and copies ran while one was open for 4% of the time, Pallas kernels for 0%

commit v1 on v0

v1 whole, which is shorter than its diff:
```python
import functools
import math

import jax
import jax.numpy as jnp
from jax import lax
from jax.experimental import pallas as pl
from jax.experimental.pallas import tpu as pltpu
from jax.sharding import PartitionSpec as P

LANES = 128
PARTS = 4


def sign_of(bits, width):
    shift = 1
    while shift < width:
        shift *= 2
    while shift > 1:
        shift //= 2
        bits = bits ^ (bits >> shift)
    return 1 - 2 * (bits & 1)


def flip_signs(rows, grad_ref, sign_ref, x_ref):
    step = min(rows, 128)
    for part in range(PARTS):
        for block in range(rows // step):
            row = part * rows + block * step
            values = grad_ref[:, pl.ds(row * LANES, step * LANES)].astype(jnp.float32)
            values = values.reshape(step, LANES)
            flips = sign_ref[pl.ds(row, step), :]
            values = jnp.where(flips == 1, -values, values)
            x_ref[pl.ds(block * step, step), pl.ds(part * LANES, LANES)] = values.astype(jnp.bfloat16)


def picked(rows, kept, x):
    picks = kept.shape[1]
    row_bits = rows.bit_length() - 1
    lane_index = kept & (LANES - 1)
    row_index = (kept >> 7) & (rows - 1)
    part_index = (kept >> (7 + row_bits)) & (PARTS - 1)
    step16 = lax.broadcasted_iota(jnp.int32, (16, picks), 0)
    table = sign_of(step16 & lane_index, 4).astype(jnp.float32).astype(jnp.bfloat16)
    bits = [(lane_index >> b) & 1 for b in range(4, 7)] + [part_index & 1, part_index >> 1]
    for bit in bits:
        factor = jnp.broadcast_to((1 - 2 * bit).astype(jnp.float32), (16, picks)).astype(jnp.bfloat16)
        factor = jnp.concatenate([factor] * (table.shape[0] // 16), axis=0)
        table = jnp.concatenate([table, table * factor], axis=0)
    total = jnp.dot(x, table, preferred_element_type=jnp.float32)
    half = rows // 2
    while half >= 8:
        bit = (row_index >> (half.bit_length() - 1)) & 1
        total = total[:half] + total[half:] * (1 - 2 * bit).astype(jnp.float32)
        half //= 2
    step8 = lax.broadcasted_iota(jnp.int32, (8, picks), 0)
    return jnp.sum(total * sign_of(step8 & row_index, 3).astype(jnp.float32), axis=0, keepdims=True)


def kernel(feats, groups, scale, grad_hbm, sign_hbm, kept_ref, query_ref, proj_ref, score_ref,
           grad, sign, x, picks, landed, queries, part, summed,
           load_sem, pick_send, pick_recv, query_send, query_recv, part_send, part_recv):
    feat = lax.axis_index("feat")
    group = lax.axis_index("grp")
    width = picks.shape[2]
    rows = x.shape[0]
    per_owner = score_ref.shape[1]

    load_grad = pltpu.make_async_copy(grad_hbm, grad, load_sem.at[0])
    load_sign = pltpu.make_async_copy(sign_hbm, sign, load_sem.at[1])
    load_grad.start()
    load_sign.start()

    barrier = pltpu.get_barrier_semaphore()

    @pl.loop(1, feats)
    def _(step):
        pl.semaphore_signal(barrier, inc=1, device_id={"feat": lax.rem(feat + step, feats)},
                            device_id_type=pl.DeviceIdType.MESH)

    @pl.loop(1, groups)
    def _(step):
        pl.semaphore_signal(barrier, inc=1, device_id={"grp": lax.rem(group + step, groups)},
                            device_id_type=pl.DeviceIdType.MESH)

    load_grad.wait()
    load_sign.wait()
    flip_signs(rows, grad, sign, x)

    pl.semaphore_wait(barrier, feats + groups - 2)

    @pl.loop(1, groups)
    def _(step):
        pltpu.make_async_remote_copy(
            src_ref=query_ref, dst_ref=queries.at[group],
            send_sem=query_send, recv_sem=query_recv,
            device_id={"grp": lax.rem(group + step, groups)}, device_id_type=pl.DeviceIdType.MESH,
        ).start()

    queries[group] = query_ref[...]

    def block(owner):
        kept = jnp.concatenate(
            [kept_ref[pl.ds(owner * (width // LANES) + i, 1), :] for i in range(width // LANES)], axis=1
        )
        sign_here = sign_of(owner & feat, feats.bit_length() - 1).astype(jnp.float32)
        return picked(rows, kept, x[...]) * (sign_here * scale)

    @pl.loop(1, feats)
    def _(step):
        owner = lax.rem(feat + step, feats)
        picks[owner] = block(owner)
        pltpu.make_async_remote_copy(
            src_ref=picks.at[owner], dst_ref=landed.at[feat],
            send_sem=pick_send, recv_sem=pick_recv,
            device_id={"feat": owner}, device_id_type=pl.DeviceIdType.MESH,
        ).start()

    landed[feat] = block(feat)

    many = picks.at[pl.ds(0, feats - 1)]
    pltpu.make_async_copy(many, many, pick_recv).wait()
    projected = jnp.sum(landed[...], axis=0).astype(jnp.bfloat16)
    proj_ref[...] = projected

    others = queries.at[pl.ds(0, groups - 1)]
    pltpu.make_async_copy(others, others, query_recv).wait()
    every = queries[...].reshape(groups * queries.shape[1], width)
    scores = lax.dot_general(projected, every, (((1,), (1,)), ((), ())), preferred_element_type=jnp.float32)
    for chunk in range(part.shape[0]):
        part[chunk] = scores[:, chunk * LANES:(chunk + 1) * LANES]

    @pl.loop(1, feats)
    def _(step):
        owner = lax.rem(feat + step, feats)
        pltpu.make_async_remote_copy(
            src_ref=part.at[owner * per_owner // LANES], dst_ref=summed.at[feat],
            send_sem=part_send, recv_sem=part_recv,
            device_id={"feat": owner}, device_id_type=pl.DeviceIdType.MESH,
        ).start()

    summed[feat] = part[feat * per_owner // LANES]
    few = summed.at[pl.ds(0, feats - 1)]
    pltpu.make_async_copy(few, few, part_recv).wait()
    total = jnp.sum(summed[...], axis=0)
    shift = LANES - lax.rem(feat * per_owner, LANES)
    total = pltpu.roll(jnp.broadcast_to(total, (8, LANES)), shift, 1)
    score_ref[...] = total[0:1, 0:per_owner]

    pltpu.make_async_copy(many, many, pick_send).wait()
    pltpu.make_async_copy(others, others, query_send).wait()
    pltpu.make_async_copy(few, few, part_send).wait()


def on_device(feats, groups, gradients, sign_bits, kept_rows, queries):
    local_len = sign_bits.shape[0]
    rows = local_len // (PARTS * LANES)
    width = kept_rows.shape[0] // feats
    all_queries = queries.shape[0] * groups
    scale = 1.0 / math.sqrt(local_len * feats)
    vmem = pl.BlockSpec(memory_space=pltpu.VMEM)
    hbm = pl.BlockSpec(memory_space=pl.ANY)
    return pl.pallas_call(
        functools.partial(kernel, feats, groups, scale),
        out_shape=(
            jax.ShapeDtypeStruct((1, width), jnp.bfloat16),
            jax.ShapeDtypeStruct((1, all_queries // feats), jnp.float32),
        ),
        in_specs=[hbm, hbm, vmem, vmem],
        out_specs=(vmem, vmem),
        scratch_shapes=[
            pltpu.VMEM((1, local_len), jnp.bfloat16),
            pltpu.VMEM((local_len // LANES, LANES), jnp.int32),
            pltpu.VMEM((rows, PARTS * LANES), jnp.bfloat16),
            pltpu.VMEM((feats, 1, width), jnp.float32),
            pltpu.VMEM((feats, 1, width), jnp.float32),
            pltpu.VMEM((groups, queries.shape[0], width), jnp.bfloat16),
            pltpu.VMEM((all_queries // LANES, 1, LANES), jnp.float32),
            pltpu.VMEM((feats, 1, LANES), jnp.float32),
            pltpu.SemaphoreType.DMA((2,)),
            pltpu.SemaphoreType.DMA,
            pltpu.SemaphoreType.DMA,
            pltpu.SemaphoreType.DMA,
            pltpu.SemaphoreType.DMA,
            pltpu.SemaphoreType.DMA,
            pltpu.SemaphoreType.DMA,
        ],
        compiler_params=pltpu.CompilerParams(
            collective_id=0, has_side_effects=True, vmem_limit_bytes=48 * 1024 * 1024
        ),
    )(gradients, sign_bits.reshape(local_len // LANES, LANES), kept_rows.reshape(-1, LANES), queries)


def solution(mesh):
    feats, groups = mesh.shape["feat"], mesh.shape["grp"]
    in_specs = (P("grp", "feat"), P("feat"), P(), P("grp", "feat"))
    out_specs = (P("grp", "feat"), P("grp", "feat"))
    return jax.shard_map(
        functools.partial(on_device, feats, groups), mesh=mesh, in_specs=in_specs, out_specs=out_specs,
        check_vma=False,
    )
```

time: 286 us -> 53.4 us (0.19)
  blocking collectives: 174 us -> 0 us
  waiting for transfers between devices: 50.6 us -> 0 us
  Pallas kernels: 0 us -> 47.4 us
  starting transfers between devices: 23.2 us -> 0 us
  other arithmetic: 19.1 us -> 0 us
  local copies, waits for them, and re-layouts: 14.1 us -> 5.11 us
  matrix products: 3.43 us -> 0 us
    unnamed x1 -> x0, blocking collectives: 141 us -> none
    ppermute x7 -> x0, waiting for transfers between devices: 50.6 us -> none  [from_behind(): lax.ppermute(array, axis, [(i, (i + by) % length) for i in range(length)])]
    pallas_call x0 -> x1, Pallas kernels: none -> 47.4 us  [on_device(): pl.pallas_call(functools.partial(kernel, feats, groups, scale), out_shape...]
    all_to_all x1 -> x0, blocking collectives: 32.4 us -> none  [on_device(): lax.all_to_all(mixed_local.reshape(examples, devices, local_len // device...]
    ppermute x7 -> x0, starting transfers between devices: 17 us -> none  [from_behind(): lax.ppermute(array, axis, [(i, (i + by) % length) for i in range(length)])]
    select_n x2 -> x0, other arithmetic: 10.1 us -> none  [the longest x1 9.29 us: on_device(): jnp.where(sign_bits == 1, -gradients, gradients)]
    unnamed x2 -> x0, other arithmetic: 7.59 us -> none
    all_to_all x1 -> x0, starting transfers between devices: 6.2 us -> none  [on_device(): lax.all_to_all(rounded, 'feat', split_axis=1, concat_axis=1, tiled=True)]
  transfers between devices with their start and end apart: 8 -> 0, of which waited for: 6 -> 0; matrix products, arithmetic and copies ran while one was open for 4% -> 0% of each run, Pallas kernels for 0% -> 0%
where the time goes in v1:
time: 53.4 us; the launch traced here: 53.1 us
  Pallas kernels  47.4 us (89%)
  local copies, waits for them, and re-layouts  5.11 us (10%)
  between operations  0.65 us (1%)
    pallas_call x1, Pallas kernels, on_device(): pl.pallas_call(functools.partial(kernel, feats, groups, scale), out_shape...  47.4 us
    unnamed x10, local copies, waits for them, and re-layouts  5.11 us

profile of v1, /device:TPU:1, one launch (start us, length us, event | category | flops | bytes accessed | tf_op | source)
XLA Modules:
  0.0 53.1 jit_solution(6906811197722433592)
XLA Ops:
  0.6 0.0 copy-start
  0.6 1.2 %copy-done = bf16[1,262144]{1,0:T(2,128)(2,1)S(1)} copy-done((bf16[1,262144]{1,0:T(2,128)(2,1)S(1)}, bf16[1,262144]{1,0:T(2,128)(2,1)}, u32[]{:S(2)}) %copy-start) | copy-done | bytes 524312
  1.9 0.0 copy-start.1
  1.9 1.2 %copy-done.1 = s32[262144]{0:T(1024)S(1)} copy-done((s32[262144]{0:T(1024)S(1)}, s32[262144]{0:T(1024)}, u32[]{:S(2)}) %copy-start.1) | copy-done | bytes 1048600
  3.1 0.0 copy-start.2
  3.1 0.8 %copy-done.2 = s32[16384]{0:T(1024)S(1)} copy-done((s32[16384]{0:T(1024)S(1)}, s32[16384]{0:T(1024)}, u32[]{:S(2)}) %copy-start.2) | copy-done | bytes 65560
  3.9 0.0 copy-start.3
  3.9 0.8 %copy-done.3 = bf16[64,256]{1,0:T(8,128)(2,1)S(1)} copy-done((bf16[64,256]{1,0:T(8,128)(2,1)S(1)}, bf16[64,256]{1,0:T(8,128)(2,1)}, u32[]{:S(2)}) %copy-start.3) | copy-done | bytes 32792
  4.7 47.4 %shard_map.59 = (bf16[1,256]{1,0:T(2,128)(2,1)S(1)}, f32[1,8]{1,0:T(1,128)S(1)}) custom-call(bf16[1,262144]{1,0:T(2,128)(2,1)S(1)} %copy-done, s32[2048,128]{1,0:T(8,128)S(1)} %bitcast.2, s32[128,128]{1,0:T(8,128)S(1)} %bitcast.3, bf16[64,256]{1,0:T(8,128)(2,1)S(1)} %copy-done.3), custom_call_target="tpu_custom_call" | custom-call | tf_op jit(solution)/shard_map/pallas_call | solution.py:163
  52.0 0.6 %copy.8 = bf16[1,256]{1,0:T(2,128)(2,1)} copy(bf16[1,256]{1,0:T(2,128)(2,1)S(1)} %get-tuple-element.4) | data formatting | bytes 1024
  52.6 0.5 copy.9
Async XLA Ops:
  0.6 1.2 %copy-start = (bf16[1,262144]{1,0:T(2,128)(2,1)S(1)}, bf16[1,262144]{1,0:T(2,128)(2,1)}, u32[]{:S(2)}) copy-start(bf16[1,262144]{1,0:T(2,128)(2,1)} %grad_hbm.1) | copy-start | bytes 1572868
  1.9 1.2 %copy-start.1 = (s32[262144]{0:T(1024)S(1)}, s32[262144]{0:T(1024)}, u32[]{:S(2)}) copy-start(s32[262144]{0:T(1024)} %param.5) | copy-start | bytes 3145732
  3.1 0.8 %copy-start.2 = (s32[16384]{0:T(1024)S(1)}, s32[16384]{0:T(1024)}, u32[]{:S(2)}) copy-start(s32[16384]{0:T(1024)} %param.6) | copy-start | bytes 196612
  3.9 0.8 %copy-start.3 = (bf16[64,256]{1,0:T(8,128)(2,1)S(1)}, bf16[64,256]{1,0:T(8,128)(2,1)}, u32[]{:S(2)}) copy-start(bf16[64,256]{1,0:T(8,128)(2,1)} %query_ref.1) | copy-start | bytes 98308

commit v2 on v1

v2 whole, which is shorter than its diff:
```python
import functools
import math

import jax
import jax.numpy as jnp
from jax import lax
from jax.experimental import pallas as pl
from jax.experimental.pallas import tpu as pltpu
from jax.sharding import PartitionSpec as P

LANES = 128
PARTS = 4
OWNERS = 8
RELAY_STEP = 4


def sign_of(bits, width):
    shift = 1
    while shift < width:
        shift *= 2
    while shift > 1:
        shift //= 2
        bits = bits ^ (bits >> shift)
    return 1 - 2 * (bits & 1)


def across(step, pairs):
    quarter = max(pairs // 4, 1)
    return lax.rem(step, pairs // quarter) * quarter + step // (pairs // quarter)


def flip_signs(part, rows, grad_ref, sign_ref, flipped_ref):
    step = min(rows, 128)
    for block in range(rows // step):
        row = part * rows + block * step
        values = grad_ref[:, pl.ds(row * LANES, step * LANES)].astype(jnp.float32)
        values = values.reshape(step, LANES)
        flips = sign_ref[pl.ds(row, step), :]
        values = jnp.where(flips == 1, -values, values)
        flipped_ref[part, pl.ds(block * step, step), :] = values.astype(jnp.bfloat16)


def picked(rows, kept, x):
    picks = kept.shape[1]
    row_bits = rows.bit_length() - 1
    lane_index = kept & (LANES - 1)
    row_index = (kept >> 7) & (rows - 1)
    part_index = (kept >> (7 + row_bits)) & (PARTS - 1)
    step16 = lax.broadcasted_iota(jnp.int32, (16, picks), 0)
    table = sign_of(step16 & lane_index, 4).astype(jnp.float32).astype(jnp.bfloat16)
    bits = [(lane_index >> b) & 1 for b in range(4, 7)] + [part_index & 1, part_index >> 1]
    for bit in bits:
        factor = jnp.broadcast_to((1 - 2 * bit).astype(jnp.float32), (16, picks)).astype(jnp.bfloat16)
        factor = jnp.concatenate([factor] * (table.shape[0] // 16), axis=0)
        table = jnp.concatenate([table, table * factor], axis=0)
    total = jnp.dot(x, table, preferred_element_type=jnp.float32)
    half = rows // 2
    while half >= 8:
        bit = (row_index >> (half.bit_length() - 1)) & 1
        total = total[:half] + total[half:] * (1 - 2 * bit).astype(jnp.float32)
        half //= 2
    step8 = lax.broadcasted_iota(jnp.int32, (8, picks), 0)
    return jnp.sum(total * sign_of(step8 & row_index, 3).astype(jnp.float32), axis=0, keepdims=True)


def main_kernel(feats, groups, owners, scale, grad_hbm, sign_hbm, kept_hbm, query_hbm, proj_ref, score_ref,
                grad, sign, kept, mine, theirs, x, picks, landed, queries, part, summed, proj, score,
                load_sem, mix_send, mix_recv, pick_send, pick_recv, near_send, near_recv, row_send, row_recv, relay_send, relay_recv,
                store_sem, part_send, part_recv):
    feat = lax.axis_index("feat")
    group = lax.axis_index("grp")
    pairs = feats // 2
    pair = feat // 2
    core = feat & 1
    width = picks.shape[2]
    rows = x.shape[0]
    per_owner = score.shape[1]
    spans = width // LANES
    mesh_ids = pl.DeviceIdType.MESH
    sibling = {"feat": feat ^ 1}
    group_rows = groups // 2

    loads = []
    for p in range(PARTS):
        lanes = pl.ds(p * rows * LANES, rows * LANES)
        span = pl.ds(p * rows, rows)
        loads.append((
            pltpu.make_async_copy(grad_hbm.at[:, lanes], grad.at[:, lanes], load_sem.at[2 * p]),
            pltpu.make_async_copy(sign_hbm.at[span], sign.at[span], load_sem.at[2 * p + 1]),
        ))
    for load_grad, load_sign in loads:
        load_grad.start()
        load_sign.start()
    load_kept = pltpu.make_async_copy(kept_hbm, kept, load_sem.at[2 * PARTS])
    load_query = pltpu.make_async_copy(query_hbm, queries.at[group], load_sem.at[2 * PARTS + 1])
    load_kept.start()
    load_query.start()

    barrier = pltpu.get_barrier_semaphore()
    pl.semaphore_signal(barrier, inc=1, device_id=sibling, device_id_type=mesh_ids)

    pl.semaphore_signal(barrier, inc=1, device_id={"grp": group ^ 1}, device_id_type=mesh_ids)

    @pl.loop(0, pairs)
    def _(step):
        other_pair = pairs - 1 - across(step, pairs)

        @pl.when(other_pair != pair)
        def _():
            pl.semaphore_signal(barrier, inc=1, device_id={"feat": 2 * other_pair + core}, device_id_type=mesh_ids)

    @pl.loop(1, group_rows)
    def _(step):
        pl.semaphore_signal(barrier, inc=1, device_id={"grp": lax.rem(group + 2 * step, groups)},
                            device_id_type=mesh_ids)

    for p, (load_grad, load_sign) in enumerate(loads):
        load_grad.wait()
        load_sign.wait()
        flip_signs(p, rows, grad, sign, mine)
    load_kept.wait()
    load_query.wait()
    pl.semaphore_wait(barrier, pairs + group_rows)

    mixes = [
        pltpu.make_async_remote_copy(
            src_ref=mine.at[p], dst_ref=theirs.at[p], send_sem=mix_send.at[p], recv_sem=mix_recv.at[p],
            device_id=sibling, device_id_type=mesh_ids,
        )
        for p in range(PARTS)
    ]
    for mix in mixes:
        mix.start()
    near = pltpu.make_async_remote_copy(
        src_ref=queries.at[group], dst_ref=queries.at[group], send_sem=near_send, recv_sem=near_recv,
        device_id={"grp": group ^ 1}, device_id_type=mesh_ids,
    )
    near.start()

    @pl.loop(1, group_rows)
    def _(other_row):
        pltpu.make_async_remote_copy(
            src_ref=queries.at[group], dst_ref=queries.at[group], send_sem=row_send, recv_sem=row_recv,
            device_id={"grp": lax.rem(group + 2 * other_row, groups)}, device_id_type=mesh_ids,
        ).start()

    own_sign = (1 - 2 * core).astype(jnp.float32)
    for p, mix in enumerate(mixes):
        mix.wait_recv()
        mixed = theirs[p].astype(jnp.float32) + mine[p].astype(jnp.float32) * own_sign
        x[:, p * LANES:(p + 1) * LANES] = mixed.astype(jnp.bfloat16)

    blocks = pairs // owners
    home = pair // owners

    for step in range(1, blocks + 1):
        first = lax.rem(home + step, blocks) * owners
        rows_kept = jnp.concatenate(
            [kept[pl.ds((2 * (first + i) + core) * spans + j, 1), :] for i in range(owners) for j in range(spans)],
            axis=1,
        )
        values = picked(rows, rows_kept, x[...])
        for i in range(owners):
            owner = first + i
            sign_here = sign_of(owner & pair, max(pairs.bit_length() - 1, 1)).astype(jnp.float32)
            picks[owner] = values[:, i * width:(i + 1) * width] * (sign_here * scale)

        @pl.loop(0, owners)
        def _(i, first=first):
            owner = first + i

            @pl.when(owner != pair)
            def _():
                pltpu.make_async_remote_copy(
                    src_ref=picks.at[owner], dst_ref=landed.at[pair],
                    send_sem=pick_send, recv_sem=pick_recv,
                    device_id={"feat": 2 * owner + core}, device_id_type=mesh_ids,
                ).start()

        if group_rows > 1 and step == min(RELAY_STEP, blocks):
            near.wait_recv()

            @pl.loop(1, group_rows)
            def _(other_row):
                pltpu.make_async_remote_copy(
                    src_ref=queries.at[group ^ 1], dst_ref=queries.at[group ^ 1],
                    send_sem=relay_send, recv_sem=relay_recv,
                    device_id={"grp": lax.rem(group + 2 * other_row, groups)}, device_id_type=mesh_ids,
                ).start()

    if group_rows == 1:
        near.wait_recv()
    landed[pair] = picks[pair]

    many = picks.at[pl.ds(0, pairs - 1)]
    pltpu.make_async_copy(many, many, pick_recv).wait()
    total = jnp.sum(landed[...], axis=0)
    projected = total.astype(jnp.bfloat16)
    proj[...] = projected
    store_proj = pltpu.make_async_copy(proj, proj_ref, store_sem.at[0])
    store_proj.start()
    rest = (total - projected.astype(jnp.float32)).astype(jnp.bfloat16)

    others = queries.at[pl.ds(0, max(group_rows - 1, 1))]
    if group_rows > 1:
        pltpu.make_async_copy(others, others, row_recv).wait()
        pltpu.make_async_copy(others, others, relay_recv).wait()
    every = queries[...].reshape(groups * queries.shape[1], width)
    scores = lax.dot_general(
        jnp.concatenate([projected, rest], axis=0), every, (((1,), (1,)), ((), ())), preferred_element_type=jnp.float32
    )
    scores = scores[0:1] + scores[1:2]
    for chunk in range(part.shape[0]):
        part[chunk] = scores[:, chunk * LANES:(chunk + 1) * LANES]
    @pl.loop(0, feats)
    def _(step):
        owner = 2 * across(step // 2, pairs) + (step & 1)

        @pl.when(owner != feat)
        def _():
            pltpu.make_async_remote_copy(
                src_ref=part.at[owner * per_owner // LANES], dst_ref=summed.at[feat],
                send_sem=part_send, recv_sem=part_recv,
                device_id={"feat": owner}, device_id_type=mesh_ids,
            ).start()

    summed[feat] = part[feat * per_owner // LANES]
    few = summed.at[pl.ds(0, feats - 1)]
    pltpu.make_async_copy(few, few, part_recv).wait()
    total = jnp.sum(summed[...], axis=0)
    shift = LANES - lax.rem(feat * per_owner, LANES)
    total = pltpu.roll(jnp.broadcast_to(total, (8, LANES)), shift, 1)
    score[...] = total[0:1, 0:per_owner]
    store_score = pltpu.make_async_copy(score, score_ref, store_sem.at[1])
    store_score.start()

    pltpu.make_async_copy(many, many, pick_send).wait()
    near.wait_send()
    if group_rows > 1:
        pltpu.make_async_copy(others, others, row_send).wait()
        pltpu.make_async_copy(others, others, relay_send).wait()
    for mix in mixes:
        mix.wait_send()
    pltpu.make_async_copy(few, few, part_send).wait()
    store_proj.wait()
    store_score.wait()


def write_kernel(proj_ref, score_ref, proj_out, score_out, sems):
    copies = [
        pltpu.make_async_copy(proj_ref, proj_out, sems.at[0]),
        pltpu.make_async_copy(score_ref, score_out, sems.at[1]),
    ]
    for copy in copies:
        copy.start()
    for copy in copies:
        copy.wait()


def on_device(feats, groups, gradients, sign_bits, kept_rows, queries):
    local_len = sign_bits.shape[0]
    rows = local_len // (PARTS * LANES)
    width = kept_rows.shape[0] // feats
    pairs = feats // 2
    all_queries = queries.shape[0] * groups
    scale = 1.0 / math.sqrt(local_len * feats)
    hbm = pl.BlockSpec(memory_space=pltpu.HBM)
    dma = pltpu.SemaphoreType.DMA
    outs = (
        jax.ShapeDtypeStruct((1, width), jnp.bfloat16),
        jax.ShapeDtypeStruct((1, all_queries // feats), jnp.float32),
    )
    projections, scores = pl.pallas_call(
        functools.partial(main_kernel, feats, groups, min(OWNERS, pairs), scale),
        out_shape=outs,
        in_specs=[hbm] * 4,
        out_specs=(hbm, hbm),
        scratch_shapes=[
            pltpu.VMEM((1, local_len), jnp.bfloat16),
            pltpu.VMEM((local_len // LANES, LANES), jnp.int32),
            pltpu.VMEM((kept_rows.shape[0] // LANES, LANES), jnp.int32),
            pltpu.VMEM((PARTS, rows, LANES), jnp.bfloat16),
            pltpu.VMEM((PARTS, rows, LANES), jnp.bfloat16),
            pltpu.VMEM((rows, PARTS * LANES), jnp.bfloat16),
            pltpu.VMEM((pairs, 1, width), jnp.float32),
            pltpu.VMEM((pairs, 1, width), jnp.float32),
            pltpu.VMEM((groups, queries.shape[0], width), jnp.bfloat16),
            pltpu.VMEM((all_queries // LANES, 1, LANES), jnp.float32),
            pltpu.VMEM((feats, 1, LANES), jnp.float32),
            pltpu.VMEM((1, width), jnp.bfloat16),
            pltpu.VMEM((1, all_queries // feats), jnp.float32),
            dma((2 * PARTS + 2,)), dma((PARTS,)), dma((PARTS,)), dma, dma, dma, dma, dma, dma, dma, dma, dma((2,)), dma, dma,
        ],
        compiler_params=pltpu.CompilerParams(
            collective_id=0, has_side_effects=True, vmem_limit_bytes=60 * 1024 * 1024
        ),
    )(gradients, sign_bits.reshape(local_len // LANES, LANES), kept_rows.reshape(-1, LANES), queries)
    return pl.pallas_call(
        write_kernel,
        out_shape=outs,
        in_specs=[hbm, hbm],
        out_specs=(hbm, hbm),
        scratch_shapes=[dma((2,))],
        compiler_params=pltpu.CompilerParams(vmem_limit_bytes=60 * 1024 * 1024),
    )(projections, scores)


def solution(mesh):
    feats, groups = mesh.shape["feat"], mesh.shape["grp"]
    in_specs = (P("grp", "feat"), P("feat"), P(), P("grp", "feat"))
    out_specs = (P("grp", "feat"), P("grp", "feat"))
    return jax.shard_map(
        functools.partial(on_device, feats, groups), mesh=mesh, in_specs=in_specs, out_specs=out_specs,
        check_vma=False,
    )
```

time: 53.4 us -> 34.8 us (0.65)
  Pallas kernels: 47.4 us -> 34 us
  local copies, waits for them, and re-layouts: 5.11 us -> 0 us
    pallas_call x1 -> x2, Pallas kernels: 47.4 us -> 34 us  [the longest x1 32.9 us: on_device(): pl.pallas_call(functools.partial(main_kernel, feats, groups, min(OWNERS,...]
    unnamed x10 -> x0, local copies, waits for them, and re-layouts: 5.11 us -> none
where the time goes in v2:
time: 34.8 us; the launch traced here: 34.7 us
  Pallas kernels  34 us (98%)
  between operations  0.64 us (2%)
    pallas_call x1, Pallas kernels, on_device(): pl.pallas_call(functools.partial(main_kernel, feats, groups, min(OWNERS,...  32.9 us
    pallas_call x1, Pallas kernels, on_device(): pl.pallas_call(write_kernel, out_shape=outs, in_specs=[hbm, hbm], out_spe...  1.17 us

profile of v2, /device:TPU:1, one launch (start us, length us, event | category | flops | bytes accessed | tf_op | source)
XLA Modules:
  0.0 34.7 jit_solution(6200016195449537470)
XLA Ops:
  0.6 32.9 %shard_map.59 = (bf16[1,256]{1,0:T(2,128)(2,1)}, f32[1,8]{1,0:T(1,128)}) custom-call(bf16[1,262144]{1,0:T(2,128)(2,1)} %grad_hbm.1, s32[2048,128]{1,0:T(8,128)} %bitcast.2, s32[128,128]{1,0:T(8,128)} %bitcast.3, bf16[64,256]{1,0:T(8,128)(2,1)} %query_hbm.1), custom_call_target="tpu_custom_call" | custom-call | tf_op jit(solution)/shard_map/pallas_call | solution.py:273
  33.5 1.2 %shard_map.60 = (bf16[1,256]{1,0:T(2,128)(2,1)}, f32[1,8]{1,0:T(1,128)}) custom-call(bf16[1,256]{1,0:T(2,128)(2,1)} %get-tuple-element.4.proj_ref, f32[1,8]{1,0:T(1,128)} %get-tuple-element.5.score_ref), custom_call_target="tpu_custom_call" | custom-call | tf_op jit(solution)/shard_map/pallas_call | solution.py:298

commit v3 on v2

v3 whole, which is shorter than its diff:
```python
import functools
import math

import jax
import jax.numpy as jnp
from jax import lax
from jax.experimental import pallas as pl
from jax.experimental.pallas import tpu as pltpu
from jax.sharding import PartitionSpec as P

LANES = 128
PARTS = 4
OWNERS = 8
ALONE_BLOCKS = 2
MAIN_VMEM = 55196 * 1024


def sign_of(bits, width):
    shift = 1
    while shift < width:
        shift *= 2
    while shift > 1:
        shift //= 2
        bits = bits ^ (bits >> shift)
    return 1 - 2 * (bits & 1)


def across(step, pairs):
    quarter = max(pairs // 4, 1)
    return lax.rem(step, pairs // quarter) * quarter + step // (pairs // quarter)


def flip_signs(part, rows, grad_ref, sign_ref, flipped_ref):
    step = min(rows, 128)
    for block in range(rows // step):
        row = part * rows + block * step
        values = grad_ref[:, pl.ds(row * LANES, step * LANES)].astype(jnp.float32)
        values = values.reshape(step, LANES)
        flips = sign_ref[pl.ds(row, step), :]
        values = jnp.where(flips == 1, -values, values)
        flipped_ref[part, pl.ds(block * step, step), :] = values.astype(jnp.bfloat16)


def picked(rows, kept, x):
    picks = kept.shape[1]
    row_bits = rows.bit_length() - 1
    lane_index = kept & (LANES - 1)
    row_index = (kept >> 7) & (rows - 1)
    part_index = (kept >> (7 + row_bits)) & (PARTS - 1)
    step16 = lax.broadcasted_iota(jnp.int32, (16, picks), 0)
    table = sign_of(step16 & lane_index, 4).astype(jnp.float32).astype(jnp.bfloat16)
    bits = [(lane_index >> b) & 1 for b in range(4, 7)] + [part_index & 1, part_index >> 1]
    for bit in bits:
        factor = jnp.broadcast_to((1 - 2 * bit).astype(jnp.float32), (16, picks)).astype(jnp.bfloat16)
        factor = jnp.concatenate([factor] * (table.shape[0] // 16), axis=0)
        table = jnp.concatenate([table, table * factor], axis=0)
    total = jnp.dot(x, table, preferred_element_type=jnp.float32)
    half = rows // 2
    while half >= 8:
        bit = (row_index >> (half.bit_length() - 1)) & 1
        total = total[:half] + total[half:] * (1 - 2 * bit).astype(jnp.float32)
        half //= 2
    step8 = lax.broadcasted_iota(jnp.int32, (8, picks), 0)
    return jnp.sum(total * sign_of(step8 & row_index, 3).astype(jnp.float32), axis=0, keepdims=True)


def main_kernel(feats, groups, owners, scale, grad_hbm, sign_hbm, kept_hbm, query_hbm, proj_ref, score_ref,
                grad, sign, kept, mine, theirs, x, picks, landed, queries, columns, part, summed,
                load_sem, mix_send, mix_recv, pick_send, pick_recv, cross_send, cross_recv, near_send, near_recv, row_send, row_recv, relay_send, relay_recv,
                part_send, part_recv):
    feat = lax.axis_index("feat")
    group = lax.axis_index("grp")
    pairs = feats // 2
    pair = feat // 2
    core = feat & 1
    width = picks.shape[3]
    rows = x.shape[0]
    per_owner = score_ref.shape[1]
    spans = width // LANES
    mesh_ids = pl.DeviceIdType.MESH
    sibling = {"feat": feat ^ 1}
    group_rows = groups // 2
    length = max(pairs // 4, 1)
    places = sorted(range(length), key=lambda z: -min(z, length - 1 - z))
    everyone = [y * length + z for z in places for y in range(pairs // length)]
    orders = [everyone[i:i + owners] for i in range(0, pairs, owners)]
    alone_blocks = min(ALONE_BLOCKS, len(orders) - 1)
    alone_owners = [owner for order in orders[:alone_blocks] for owner in order]
    in_first = functools.reduce(jnp.logical_or, [pair == owner for owner in alone_owners])
    landed[1] = jnp.zeros_like(landed[1])

    loads = []
    for p in range(PARTS):
        lanes = pl.ds(p * rows * LANES, rows * LANES)
        span = pl.ds(p * rows, rows)
        loads.append((
            pltpu.make_async_copy(grad_hbm.at[:, lanes], grad.at[:, lanes], load_sem.at[2 * p]),
            pltpu.make_async_copy(sign_hbm.at[span], sign.at[span], load_sem.at[2 * p + 1]),
        ))
    for load_grad, load_sign in loads:
        load_grad.start()
        load_sign.start()
    load_kept = pltpu.make_async_copy(kept_hbm, kept, load_sem.at[2 * PARTS])
    load_query = pltpu.make_async_copy(query_hbm, queries.at[group], load_sem.at[2 * PARTS + 1])
    load_kept.start()
    load_query.start()

    barrier = pltpu.get_barrier_semaphore()
    pl.semaphore_signal(barrier, inc=1, device_id=sibling, device_id_type=mesh_ids)

    pl.semaphore_signal(barrier, inc=1, device_id={"grp": group ^ 1}, device_id_type=mesh_ids)

    @pl.loop(0, pairs)
    def _(step):
        other_pair = across(step, pairs)

        @pl.when(other_pair != pair)
        def _():
            pl.semaphore_signal(barrier, inc=1, device_id={"feat": 2 * other_pair + core}, device_id_type=mesh_ids)

    @pl.loop(1, group_rows)
    def _(step):
        pl.semaphore_signal(barrier, inc=1, device_id={"grp": lax.rem(group + 2 * step, groups)},
                            device_id_type=mesh_ids)

    for p, (load_grad, load_sign) in enumerate(loads):
        load_grad.wait()
        load_sign.wait()
        flip_signs(p, rows, grad, sign, mine)
    load_kept.wait()
    load_query.wait()

    def compute(order, table, side, unmixed):
        owner_core = core ^ side
        rows_kept = jnp.concatenate(
            [kept[pl.ds((2 * owner + owner_core) * spans + j, 1), :] for owner in order for j in range(spans)], axis=1
        )
        values = picked(rows, rows_kept, table)
        pair_bits = max(pairs.bit_length() - 1, 1)
        for i, owner in enumerate(order):
            factor = sign_of(owner & pair, pair_bits).astype(jnp.float32) * scale
            if unmixed:
                factor = factor * (1 - 2 * (core & owner_core)).astype(jnp.float32)
            picks[side, owner] = values[:, i * width:(i + 1) * width] * factor

    def send_own(order):
        for owner in order:
            @pl.when(owner != pair)
            def _(owner=owner):
                pltpu.make_async_remote_copy(
                    src_ref=picks.at[0, owner], dst_ref=landed.at[0, pair], send_sem=pick_send, recv_sem=pick_recv,
                    device_id={"feat": 2 * owner + core}, device_id_type=mesh_ids,
                ).start()

    def relay():
        near.wait_recv()

        @pl.loop(1, group_rows)
        def _(other_row):
            pltpu.make_async_remote_copy(
                src_ref=queries.at[group ^ 1], dst_ref=queries.at[group ^ 1],
                send_sem=relay_send, recv_sem=relay_recv,
                device_id={"grp": lax.rem(group + 2 * other_row, groups)}, device_id_type=mesh_ids,
            ).start()

    mixes = [
        pltpu.make_async_remote_copy(
            src_ref=mine.at[p], dst_ref=theirs.at[p], send_sem=mix_send.at[p], recv_sem=mix_recv.at[p],
            device_id=sibling, device_id_type=mesh_ids,
        )
        for p in range(PARTS)
    ]
    near = pltpu.make_async_remote_copy(
        src_ref=queries.at[group], dst_ref=queries.at[group], send_sem=near_send, recv_sem=near_recv,
        device_id={"grp": group ^ 1}, device_id_type=mesh_ids,
    )

    def open_links():
        pl.semaphore_wait(barrier, pairs + group_rows)
        near.start()
        for mix in mixes:
            mix.start()

        @pl.loop(1, group_rows)
        def _(other_row):
            pltpu.make_async_remote_copy(
                src_ref=queries.at[group], dst_ref=queries.at[group], send_sem=row_send, recv_sem=row_recv,
                device_id={"grp": lax.rem(group + 2 * other_row, groups)}, device_id_type=mesh_ids,
            ).start()

    alone = jnp.concatenate([mine[p] for p in range(PARTS)], axis=1)
    far_half = lax.rem(pair, length) >= length // 2
    for step, order in enumerate(orders[:alone_blocks]):
        compute(order, alone, 0, True)
        compute(order, alone, 1, True)
        if step == 0:
            pl.when(far_half)(open_links)
    pl.when(jnp.logical_not(far_half))(open_links)
    for order in orders[:alone_blocks]:
        send_own(order)
    own_sign = (1 - 2 * core).astype(jnp.float32)
    for p, mix in enumerate(mixes):
        mix.wait_recv()
        mixed = theirs[p].astype(jnp.float32) + mine[p].astype(jnp.float32) * own_sign
        x[:, p * LANES:(p + 1) * LANES] = mixed.astype(jnp.bfloat16)

    for owner in alone_owners:
        pltpu.make_async_remote_copy(
            src_ref=picks.at[1, owner], dst_ref=landed.at[1, pair], send_sem=cross_send, recv_sem=cross_recv,
            device_id={"feat": 2 * owner + 1 - core}, device_id_type=mesh_ids,
        ).start()

    for step, order in enumerate(orders[alone_blocks:]):
        compute(order, x[...], 0, False)
        send_own(order)

    landed[0, pair] = picks[0, pair]

    def lay_out(side):
        blocks = [queries[2 * row + side] for row in range(group_rows)]
        return jnp.concatenate(blocks, axis=0).astype(jnp.float32).T.astype(jnp.bfloat16)

    side = group & 1
    others = queries.at[pl.ds(0, max(group_rows - 1, 1))]

    def take_own_side():
        if group_rows > 1:
            pltpu.make_async_copy(others, others, row_recv).wait()

    def take_other_side():
        if group_rows > 1:
            pltpu.make_async_copy(others, others, relay_recv).wait()

    relay()
    pl.when(side == 0)(take_own_side)
    pl.when(side == 1)(take_other_side)
    columns[...] = lay_out(0)

    many = picks.at[0, pl.ds(0, pairs - 1)]
    crossed = picks.at[0]
    pltpu.make_async_copy(many, many, pick_recv).wait()

    @pl.when(in_first)
    def _():
        pltpu.make_async_copy(crossed, crossed, cross_recv).wait()

    total = jnp.sum(landed[0] + landed[1], axis=0)
    projected = total.astype(jnp.bfloat16)
    proj_ref[...] = projected
    rest = (total - projected.astype(jnp.float32)).astype(jnp.bfloat16)
    both = jnp.concatenate([projected, rest], axis=0)
    per_group = queries.shape[1] // per_owner

    def place(owner):
        return owner // (2 * per_group) * queries.shape[1] + lax.rem(owner, per_group) * per_owner

    def send_scores(turn, query_side):
        scores = jnp.dot(both, columns[...], preferred_element_type=jnp.float32)
        scores = scores[0:1] + scores[1:2]
        for chunk in range(part.shape[1]):
            part[turn, chunk] = scores[:, chunk * LANES:(chunk + 1) * LANES]

        @pl.loop(0, feats)
        def _(step):
            owner = 2 * across(step // 2, pairs) + (step & 1)
            on_side = (owner // per_group) & 1 == query_side

            @pl.when(jnp.logical_and(on_side, owner != feat))
            def _():
                pltpu.make_async_remote_copy(
                    src_ref=part.at[turn, place(owner) // LANES], dst_ref=summed.at[feat],
                    send_sem=part_send, recv_sem=part_recv,
                    device_id={"feat": owner}, device_id_type=mesh_ids,
                ).start()

            @pl.when(jnp.logical_and(on_side, owner == feat))
            def _():
                summed[feat] = part[turn, place(owner) // LANES]

    send_scores(0, 0)
    pl.when(side == 1)(take_own_side)
    pl.when(side == 0)(take_other_side)
    columns[...] = lay_out(1)
    send_scores(1, 1)

    few = summed.at[pl.ds(0, feats - 1)]
    pltpu.make_async_copy(few, few, part_recv).wait()
    total = jnp.sum(summed[...], axis=0)
    shift = LANES - lax.rem(place(feat), LANES)
    total = pltpu.roll(jnp.broadcast_to(total, (8, LANES)), shift, 1)
    score_ref[...] = total[0:1, 0:per_owner]

    pltpu.make_async_copy(many, many, pick_send).wait()
    gone = picks.at[0, pl.ds(0, len(alone_owners))]
    pltpu.make_async_copy(gone, gone, cross_send).wait()
    near.wait_send()
    if group_rows > 1:
        pltpu.make_async_copy(others, others, row_send).wait()
        pltpu.make_async_copy(others, others, relay_send).wait()
    for mix in mixes:
        mix.wait_send()
    pltpu.make_async_copy(few, few, part_send).wait()


def write_kernel(proj_ref, score_ref, proj_out, score_out, sems):
    copies = [
        pltpu.make_async_copy(proj_ref, proj_out, sems.at[0]),
        pltpu.make_async_copy(score_ref, score_out, sems.at[1]),
    ]
    for copy in copies:
        copy.start()
    for copy in copies:
        copy.wait()


def on_device(feats, groups, gradients, sign_bits, kept_rows, queries):
    local_len = sign_bits.shape[0]
    rows = local_len // (PARTS * LANES)
    width = kept_rows.shape[0] // feats
    pairs = feats // 2
    all_queries = queries.shape[0] * groups
    scale = 1.0 / math.sqrt(local_len * feats)
    hbm = pl.BlockSpec(memory_space=pltpu.HBM)
    vmem = pl.BlockSpec(memory_space=pltpu.VMEM)
    dma = pltpu.SemaphoreType.DMA
    outs = (
        jax.ShapeDtypeStruct((1, width), jnp.bfloat16),
        jax.ShapeDtypeStruct((1, all_queries // feats), jnp.float32),
    )
    projections, scores = pl.pallas_call(
        functools.partial(main_kernel, feats, groups, min(OWNERS, pairs // 2), scale),
        out_shape=outs,
        in_specs=[hbm] * 4,
        out_specs=(vmem, vmem),
        scratch_shapes=[
            pltpu.VMEM((1, local_len), jnp.bfloat16),
            pltpu.VMEM((local_len // LANES, LANES), jnp.int32),
            pltpu.VMEM((kept_rows.shape[0] // LANES, LANES), jnp.int32),
            pltpu.VMEM((PARTS, rows, LANES), jnp.bfloat16),
            pltpu.VMEM((PARTS, rows, LANES), jnp.bfloat16),
            pltpu.VMEM((rows, PARTS * LANES), jnp.bfloat16),
            pltpu.VMEM((2, pairs, 1, width), jnp.float32),
            pltpu.VMEM((2, pairs, 1, width), jnp.float32),
            pltpu.VMEM((groups, queries.shape[0], width), jnp.bfloat16),
            pltpu.VMEM((width, all_queries // 2), jnp.bfloat16),
            pltpu.VMEM((2, all_queries // (2 * LANES), 1, LANES), jnp.float32),
            pltpu.VMEM((feats, 1, LANES), jnp.float32),
            dma((2 * PARTS + 2,)), dma((PARTS,)), dma((PARTS,)), dma, dma, dma, dma, dma, dma, dma, dma, dma, dma, dma, dma,
        ],
        compiler_params=pltpu.CompilerParams(
            collective_id=0, has_side_effects=True, vmem_limit_bytes=MAIN_VMEM
        ),
    )(gradients, sign_bits.reshape(local_len // LANES, LANES), kept_rows.reshape(-1, LANES), queries)
    return pl.pallas_call(
        write_kernel,
        out_shape=outs,
        in_specs=[vmem, vmem],
        out_specs=(hbm, hbm),
        scratch_shapes=[dma((2,))],
        compiler_params=pltpu.CompilerParams(vmem_limit_bytes=8 * 1024 * 1024),
    )(projections, scores)


def solution(mesh):
    feats, groups = mesh.shape["feat"], mesh.shape["grp"]
    in_specs = (P("grp", "feat"), P("feat"), P(), P("grp", "feat"))
    out_specs = (P("grp", "feat"), P("grp", "feat"))
    return jax.shard_map(
        functools.partial(on_device, feats, groups), mesh=mesh, in_specs=in_specs, out_specs=out_specs,
        check_vma=False,
    )
```

time: 34.8 us -> 32.5 us (0.934); the launches traced: 34.7 us -> 32 us
  Pallas kernels: 34 us -> 31.3 us
    pallas_call x1, Pallas kernels: 32.9 us -> 30.8 us  [on_device(): pl.pallas_call(functools.partial(main_kernel, feats, groups, min(OWNERS,...]
    pallas_call x1, Pallas kernels: 1.17 us -> 0.58 us  [on_device(): pl.pallas_call(write_kernel, out_shape=outs, in_specs=[vmem, vmem], out_s...]
where the time goes in v3:
time: 32.5 us; the launch traced here: 32 us
  Pallas kernels  31.3 us (96%)
  between operations  0.64 us (2%)
    pallas_call x1, Pallas kernels, on_device(): pl.pallas_call(functools.partial(main_kernel, feats, groups, min(OWNERS,...  30.8 us

profile of v3, /device:TPU:1, one launch (start us, length us, event | category | flops | bytes accessed | tf_op | source)
XLA Modules:
  0.0 32.0 jit_solution(2423786962914980757)
XLA Ops:
  0.6 30.8 %shard_map.59 = (bf16[1,256]{1,0:T(2,128)(2,1)S(1)}, f32[1,8]{1,0:T(1,128)S(1)}) custom-call(bf16[1,262144]{1,0:T(2,128)(2,1)} %grad_hbm.1, s32[2048,128]{1,0:T(8,128)} %bitcast.2, s32[128,128]{1,0:T(8,128)} %bitcast.3, bf16[64,256]{1,0:T(8,128)(2,1)} %query_hbm.1), custom_call_target="tpu_custom_call" | custom-call | tf_op jit(solution)/shard_map/pallas_call | solution.py:330
  31.4 0.6 %shard_map.60 = (bf16[1,256]{1,0:T(2,128)(2,1)}, f32[1,8]{1,0:T(1,128)}) custom-call(bf16[1,256]{1,0:T(2,128)(2,1)S(1)} %get-tuple-element.4.proj_ref, f32[1,8]{1,0:T(1,128)S(1)} %get-tuple-element.5.score_ref), custom_call_target="tpu_custom_call" | custom-call | tf_op jit(solution)/shard_map/pallas_call | solution.py:354
